TPU v7x, 32 devices: a whole 2x2x4 slice. The times are simulated.
32 devices in a mesh: group: 2 (over y), expert: 4 (over x, core), dp: 4 (over z).
Axes of the slice: x: 2, y: 2, z: 4, core: 2. Of those that a mesh axis runs over, the one named last changes fastest.
Arguments:
- cotangent: bfloat16 [8192, 7168], P(('group', 'expert', 'dp')), parts along dimension 0, may hold values from -6 to 6
- expert_ids: int32 [8192, 8], P(('group', 'expert', 'dp')), parts along dimension 0, may hold values from 0 to 255, all different within a row; in each aligned block of 128 rows (0 to 127, 128 to 255, ...) at most 8 rows name the same one
- gate_values: float32 [8192, 8], P(('group', 'expert', 'dp')), parts along dimension 0, may hold values from 0.02 to 0.3
- hidden: bfloat16 [8, 4, 4, 2, 8, 1024], P(('group', 'expert'), 'dp'), parts along dimension 0, may hold values from -6 to 6
- down_weight: bfloat16 [4, 1024, 7168], P('expert', None, 'dp'), may hold values from -0.1875 to 0.1875
Outputs:
- fisher: float32 [8, 1024, 7168], P(('group', 'expert'), None, 'dp'), parts along dimension 0
- hidden_grad: bfloat16 [8, 4, 4, 2, 8, 1024], P(('group', 'expert'), 'dp'), parts along dimension 0
There are 2 independent parts, one for each index of `group`. A program takes and returns all parts, laid end to end along the dimension named above; an argument that names none is the same for every part. Nothing has to cross between parts.
Inputs may be any that keep to these rules, and one draw needn't show every extreme that they name: `expert_ids`: each token names 8 different experts. In each aligned block of 128 tokens no expert is named by more than 8 tokens, a bound that some block reaches.
All inputs are finite; a program needn't handle non-finite values.
Results may differ from a plain program's by a relative error of at most 0.0051.
Values may be sent and summed in bfloat16 or wider, within the bound.
A program may use at most 128 MiB of HBM per device.

v0:
```python
import jax
import jax.numpy as jnp
from jax import lax
from jax.sharding import PartitionSpec as P

GROUP = 128


def per_device(cotangent, expert_ids, gate_values, hidden, down_weight):
    experts = lax.axis_size("expert")
    ways = lax.axis_size("dp")
    width = cotangent.shape[1]
    capacity = hidden.shape[4]
    groups_dev = hidden.shape[3]
    hidden_units = hidden.shape[5]
    window = jnp.arange(experts, dtype=jnp.int32)
    match = expert_ids[:, :, None] == window[None, None, :]
    chosen = jnp.any(match, axis=1).astype(jnp.int32).reshape(groups_dev, GROUP, experts)
    weight_sel = jnp.sum(jnp.where(match, gate_values[:, :, None], jnp.float32(0.0)), axis=1)
    weight_sel = weight_sel.reshape(groups_dev, GROUP, experts)
    rank = jnp.cumsum(chosen, axis=1) - 1
    slots = jnp.arange(capacity, dtype=jnp.int32)
    place = (rank[..., None] == slots) & (chosen[..., None] == 1)
    slot_gate = jnp.sum(jnp.where(place, weight_sel[..., None], jnp.float32(0.0)), axis=1)
    token_rows = cotangent.reshape(groups_dev, GROUP, width)
    picked = jnp.einsum(
        "jgec,jgd->ejcd", place.astype(jnp.bfloat16), token_rows, preferred_element_type=jnp.float32
    )
    routed = (picked * jnp.transpose(slot_gate, (1, 0, 2))[..., None]).astype(jnp.bfloat16)
    columns = lax.all_to_all(
        lax.all_to_all(routed[None], "expert", split_axis=1, concat_axis=1, tiled=True),
        "dp",
        split_axis=4,
        concat_axis=0,
        tiled=True,
    )
    flat_cols = columns.reshape(-1, columns.shape[4])
    grad_rows = lax.psum_scatter(
        lax.dot_general(
            flat_cols, down_weight[0], (((1,), (1,)), ((), ())), preferred_element_type=jnp.float32
        ),
        "dp",
        scatter_dimension=0,
        tiled=True,
    )
    hidden_grad = grad_rows.astype(jnp.bfloat16).reshape(hidden.shape)
    shard_width = columns.shape[4]
    empty_fisher = jnp.zeros((hidden_units, shard_width), jnp.float32)
    piece = lax.all_gather(hidden, "dp", axis=1, tiled=True)
    count = piece.shape[1]

    def turn(index, accum):
        source = index // groups_dev
        block = index % groups_dev
        block_h = lax.dynamic_index_in_dim(piece[0], source, 0, keepdims=False)
        block_h = lax.dynamic_index_in_dim(block_h, block, 1, keepdims=False).reshape(
            -1, hidden_units
        )
        block_c = lax.dynamic_index_in_dim(columns, source, 0, keepdims=False)
        block_c = lax.dynamic_index_in_dim(block_c, block, 1, keepdims=False).reshape(
            -1, shard_width
        )
        prod = lax.dot_general(
            block_h, block_c, (((0,), (0,)), ((), ())), preferred_element_type=jnp.float32
        )
        return accum + prod * prod

    fisher_sum = lax.fori_loop(0, count * groups_dev, turn, empty_fisher)
    fisher = (fisher_sum * (1.0 / (ways * groups_dev)))[None]
    return (fisher, hidden_grad)


def solution(mesh):
    in_specs = (
        P(("group", "expert", "dp"), None),
        P(("group", "expert", "dp"), None),
        P(("group", "expert", "dp"), None),
        P(("group", "expert"), "dp", None, None, None, None),
        P("expert", None, "dp"),
    )
    out_specs = (
        P(("group", "expert"), None, "dp"),
        P(("group", "expert"), "dp", None, None, None, None),
    )
    return jax.shard_map(
        per_device, mesh=mesh, in_specs=in_specs, out_specs=out_specs, check_vma=False
    )
```

profile of v0, /device:TPU:0, one launch (start us, length us, event | category | flops | bytes accessed | tf_op | source)
XLA Modules:
  0.0 210.9 jit_solution(8177170741901431970)
XLA Ops:
  7.2 0.7 fusion.10
  7.9 0.1 copy.27
  8.1 0.2 reduce_window_sum.11
  8.3 0.1 copy.28
  8.4 0.7 select_reduce_fusion.1
  9.1 0.1 select_reduce_fusion
  9.2 2.6 %fusion.7 = bf16[1,4,2,8,7168]{4,3,1,2,0:T(8,128)(2,1)S(1)} fusion(bf16[2,128,7168,1]{2,1,3,0:T(8,128)(2,1)} %bitcast.49, f32[4,2,8]{2,0,1:T(4,128)S(1)} %bitcast.55, s32[2,128,4]{1,2,0:T(4,128)S(1)} %copy.28, pred[2,128,4]{1,2,0:T(4,128)(4,1)S(1)} %copy.29), kind=kOutput, calls=%fused_computation.9 | convolution fusion | flops 118374400 | bytes 4592896 | tf_op jit(solution)/shard_map/jgec,jgd->ejcd/dot_general | solution.py:26
  11.8 0.1 copy.30
  11.9 17.1 %all_to_all.23 = bf16[1,4,2,8,7168]{4,3,2,0,1:T(8,128)(2,1)S(1)} all-to-all(bf16[1,4,2,8,7168]{4,3,2,0,1:T(8,128)(2,1)S(1)} %copy.30), channel_id=1, replica_groups=mesh['group'=2,'expert'=4,'dp'=4] {'expert'}, dimensions={1} | all-to-all | bytes 1835008 | tf_op jit(solution)/shard_map/all_to_all | solution.py:31
  29.0 14.6 %copy.31 = bf16[1,4,2,8,7168]{3,1,2,0,4:T(4,128)(2,1)} copy(bf16[1,4,2,8,7168]{4,3,2,0,1:T(8,128)(2,1)S(1)} %all_to_all.23) | data formatting | bytes 1835008 | tf_op jit(solution)/shard_map/all_to_all | solution.py:31
  43.6 0.0 copy-start
  43.6 18.8 %reshape.79 = bf16[4,2,57344]{2,1,0:T(2,128)(2,1)} reshape(bf16[7168,1,2,4,8]{4,3,2,1,0:T(4,128)(2,1)} %bitcast.47) | data formatting | bytes 1835008
  62.4 4.9 %all-to-all-start.1 = ((bf16[4,2,57344]{2,1,0:T(2,128)(2,1)}), bf16[4,2,57344]{2,1,0:T(2,128)(2,1)S(1)}, u32[]{:S(2)}, u32[]{:S(2)}) async-start(bf16[4,2,57344]{2,1,0:T(2,128)(2,1)} %reshape.79), calls=%async_computation.1 | async-start | bytes 1835008 | tf_op jit(solution)/shard_map/all_to_all | solution.py:30
  67.2 0.0 reduce-scatter.2.cloned.1.call-start
  67.2 0.0 copy-done
  67.3 32.4 %all_gather.3 = bf16[1,4,4,2,8,1024]{5,4,3,2,0,1:T(8,128)(2,1)S(1)} all-gather(bf16[1,1,4,2,8,1024]{5,4,3,2,0,1:T(8,128)(2,1)S(1)} %bitcast.53), channel_id=1, replica_groups=mesh['group'=2,'expert'=4,'dp'=4] {'dp'}, dimensions={1}, use_global_device_ids=true | all-gather | bytes 655360 | tf_op jit(solution)/shard_map/all_gather | solution.py:49
  99.7 0.0 all-to-all-done.1
  99.7 19.4 %reshape.80 = bf16[7168,1,2,4,8]{4,3,2,1,0:T(4,128)(2,1)} reshape(bf16[4,2,57344]{2,1,0:T(2,128)(2,1)S(1)} %all-to-all-done.1) | data formatting | bytes 1835008
  119.0 17.1 %copy.32 = bf16[1,4,2,8,4,1792]{5,3,2,1,4,0:T(8,128)(2,1)S(1)} copy(bf16[1,4,2,8,4,1792]{3,1,2,5,4,0:T(4,128)(2,1)} %bitcast.48) | data formatting | bytes 1835008 | tf_op jit(solution)/shard_map/all_to_all | solution.py:30
  136.2 4.2 %fusion.8 = f32[256,1024]{1,0:T(8,128)} fusion(bf16[256,1792]{1,0:T(8,128)(2,1)S(1)} %bitcast.50, bf16[1,1024,1792]{2,1,0:T(8,128)(2,1)} %param.11), kind=kOutput, calls=%fused_computation.11 | convolution fusion | flops 939524096 | bytes 5636096 | tf_op jit(solution)/shard_map/dot_general | solution.py:39
  140.4 0.0 reduce-scatter.2.cloned.1.call-update
  140.4 55.5 %while.17 = (s32[]{:T(128)}, f32[1024,1792]{1,0:T(8,128)}, bf16[1,4,4,2,8,1024]{5,4,3,2,1,0:T(8,128)(2,1)S(1)}, bf16[4,4,2,8,1792]{4,3,2,1,0:T(8,128)(2,1)S(1)},...) while((s32[]{:T(128)}, f32[1024,1792]{1,0:T(8,128)}, ...), condition=%wide.region_5.6_spmd.clone, body=%wide.region_4.5_spmd.clone.sunk | while | flops 122945560 | bytes 14863173 | solution.py:68
  140.4 4.2 %select_add_fusion.2 = f32[1024,1792]{1,0:T(8,128)} fusion(f32[1024,1792]{1,0:T(8,128)} %get-tuple-element.208, pred[]{:T(512)S(6)} %compare.16, bf16[4,4,2,8,1792]{4,3,2,1,0:T(8,128)(2,1)S(1)} %get-tuple-element.220, s32[]{:T(128)S(6)} %select_n.92, s32[]{:T(128)S(6)} %select_n.95, bf16[1,4,4,2,8,1024]{5,4,3,2,1,0:T(8,128)(2,1)S(1)} %get-tuple-element.219), kind=kOutput, calls=%fused_computation.clone.1 | convolution fusion | flops 122945536 | bytes 14862848 | tf_op jit(solution)/shard_map/while/body/eval_jaxpr/dot_general | solution.py:63
  144.6 7.4 %select_add_fusion.2 = f32[1024,1792]{1,0:T(8,128)} fusion(f32[1024,1792]{1,0:T(8,128)} %get-tuple-element.208, pred[]{:T(512)S(6)} %compare.16, bf16[4,4,2,8,1792]{4,3,2,1,0:T(8,128)(2,1)S(1)} %get-tuple-element.220, s32[]{:T(128)S(6)} %select_n.92, s32[]{:T(128)S(6)} %select_n.95, bf16[1,4,4,2,8,1024]{5,4,3,2,1,0:T(8,128)(2,1)S(1)} %get-tuple-element.219), kind=kOutput, calls=%fused_computation.clone.1 | convolution fusion | flops 122945536 | bytes 14862848 | tf_op jit(solution)/shard_map/while/body/eval_jaxpr/dot_general | solution.py:63
  152.1 7.3 %select_add_fusion.2 = f32[1024,1792]{1,0:T(8,128)} fusion(f32[1024,1792]{1,0:T(8,128)} %get-tuple-element.208, pred[]{:T(512)S(6)} %compare.16, bf16[4,4,2,8,1792]{4,3,2,1,0:T(8,128)(2,1)S(1)} %get-tuple-element.220, s32[]{:T(128)S(6)} %select_n.92, s32[]{:T(128)S(6)} %select_n.95, bf16[1,4,4,2,8,1024]{5,4,3,2,1,0:T(8,128)(2,1)S(1)} %get-tuple-element.219), kind=kOutput, calls=%fused_computation.clone.1 | convolution fusion | flops 122945536 | bytes 14862848 | tf_op jit(solution)/shard_map/while/body/eval_jaxpr/dot_general | solution.py:63
  159.4 7.3 %select_add_fusion.2 = f32[1024,1792]{1,0:T(8,128)} fusion(f32[1024,1792]{1,0:T(8,128)} %get-tuple-element.208, pred[]{:T(512)S(6)} %compare.16, bf16[4,4,2,8,1792]{4,3,2,1,0:T(8,128)(2,1)S(1)} %get-tuple-element.220, s32[]{:T(128)S(6)} %select_n.92, s32[]{:T(128)S(6)} %select_n.95, bf16[1,4,4,2,8,1024]{5,4,3,2,1,0:T(8,128)(2,1)S(1)} %get-tuple-element.219), kind=kOutput, calls=%fused_computation.clone.1 | convolution fusion | flops 122945536 | bytes 14862848 | tf_op jit(solution)/shard_map/while/body/eval_jaxpr/dot_general | solution.py:63
  166.7 7.3 %select_add_fusion.2 = f32[1024,1792]{1,0:T(8,128)} fusion(f32[1024,1792]{1,0:T(8,128)} %get-tuple-element.208, pred[]{:T(512)S(6)} %compare.16, bf16[4,4,2,8,1792]{4,3,2,1,0:T(8,128)(2,1)S(1)} %get-tuple-element.220, s32[]{:T(128)S(6)} %select_n.92, s32[]{:T(128)S(6)} %select_n.95, bf16[1,4,4,2,8,1024]{5,4,3,2,1,0:T(8,128)(2,1)S(1)} %get-tuple-element.219), kind=kOutput, calls=%fused_computation.clone.1 | convolution fusion | flops 122945536 | bytes 14862848 | tf_op jit(solution)/shard_map/while/body/eval_jaxpr/dot_general | solution.py:63
  174.0 7.3 %select_add_fusion.2 = f32[1024,1792]{1,0:T(8,128)} fusion(f32[1024,1792]{1,0:T(8,128)} %get-tuple-element.208, pred[]{:T(512)S(6)} %compare.16, bf16[4,4,2,8,1792]{4,3,2,1,0:T(8,128)(2,1)S(1)} %get-tuple-element.220, s32[]{:T(128)S(6)} %select_n.92, s32[]{:T(128)S(6)} %select_n.95, bf16[1,4,4,2,8,1024]{5,4,3,2,1,0:T(8,128)(2,1)S(1)} %get-tuple-element.219), kind=kOutput, calls=%fused_computation.clone.1 | convolution fusion | flops 122945536 | bytes 14862848 | tf_op jit(solution)/shard_map/while/body/eval_jaxpr/dot_general | solution.py:63
  181.3 7.3 %select_add_fusion.2 = f32[1024,1792]{1,0:T(8,128)} fusion(f32[1024,1792]{1,0:T(8,128)} %get-tuple-element.208, pred[]{:T(512)S(6)} %compare.16, bf16[4,4,2,8,1792]{4,3,2,1,0:T(8,128)(2,1)S(1)} %get-tuple-element.220, s32[]{:T(128)S(6)} %select_n.92, s32[]{:T(128)S(6)} %select_n.95, bf16[1,4,4,2,8,1024]{5,4,3,2,1,0:T(8,128)(2,1)S(1)} %get-tuple-element.219), kind=kOutput, calls=%fused_computation.clone.1 | convolution fusion | flops 122945536 | bytes 14862848 | tf_op jit(solution)/shard_map/while/body/eval_jaxpr/dot_general | solution.py:63
  188.6 7.3 %select_add_fusion.2 = f32[1024,1792]{1,0:T(8,128)} fusion(f32[1024,1792]{1,0:T(8,128)} %get-tuple-element.208, pred[]{:T(512)S(6)} %compare.16, bf16[4,4,2,8,1792]{4,3,2,1,0:T(8,128)(2,1)S(1)} %get-tuple-element.220, s32[]{:T(128)S(6)} %select_n.92, s32[]{:T(128)S(6)} %select_n.95, bf16[1,4,4,2,8,1024]{5,4,3,2,1,0:T(8,128)(2,1)S(1)} %get-tuple-element.219), kind=kOutput, calls=%fused_computation.clone.1 | convolution fusion | flops 122945536 | bytes 14862848 | tf_op jit(solution)/shard_map/while/body/eval_jaxpr/dot_general | solution.py:63
  195.9 6.6 %multiply_bitcast_fusion = f32[1,1024,1792]{2,1,0:T(8,128)} fusion(f32[1024,1792]{1,0:T(8,128)} %get-tuple-element.140), kind=kLoop, calls=%fused_computation.10 | loop fusion | flops 1835008 | bytes 14680064 | tf_op jit(solution)/shard_map/broadcast_in_dim | solution.py:69
  202.5 1.6 convert_element_type.26
  (7 shorter events, 0.0 us)
Async XLA Ops:
  43.6 23.7 %copy-start = (bf16[1,1,4,2,8,1024]{5,4,3,2,1,0:T(8,128)(2,1)S(1)}, bf16[1,1,4,2,8,1024]{5,4,3,2,1,0:T(8,128)(2,1)}, u32[]{:S(2)}) copy-start(bf16[1,1,4,2,8,1024]{5,4,3,2,1,0:T(8,128)(2,1)} %param.10) | copy-start | bytes 393220
  62.4 37.3 %all-to-all-start.1 = ((bf16[4,2,57344]{2,1,0:T(2,128)(2,1)}), bf16[4,2,57344]{2,1,0:T(2,128)(2,1)S(1)}, u32[]{:S(2)}, u32[]{:S(2)}) async-start(bf16[4,2,57344]{2,1,0:T(2,128)(2,1)} %reshape.79), calls=%async_computation.1 | async-start | bytes 1835008 | tf_op jit(solution)/shard_map/all_to_all | solution.py:30
  67.2 135.2 %reduce-scatter.2.cloned.1.call-start = ((), (), s32[]{:S(2)}) async-start(), calls=%async_computation.3 | async-start | bytes 1310720 | tf_op jit(solution)/shard_map/reduce_scatter | solution.py:38
Sparse Core Ops, SparseCore 0:
  140.5 27.8 reduce-scatter.1
where the time goes:
time: 212 us; the launch traced here: 211 us
  local copies, waits for them, and re-layouts  70.2 us (33%)
  matrix products  62.3 us (29%)
  blocking collectives  49.5 us (23%)
  between operations  14.1 us (7%)
  other arithmetic  10 us (5%)
  starting transfers between devices  4.87 us (2%)
    dot_general x8, matrix products, turn(): lax.dot_general(block_h, block_c, (((0,), (0,)), ((), ())), preferred_ele...  55.4 us
    unnamed x4, local copies, waits for them, and re-layouts  38.2 us
    all_gather x1, blocking collectives, per_device(): piece = lax.all_gather(hidden, 'dp', axis=1, tiled=True)  32.4 us
    all_to_all x1, local copies, waits for them, and re-layouts, per_device(): lax.all_to_all(lax.all_to_all(routed[None], 'expert', split_axis=1, conca...  17.1 us
    all_to_all x1, blocking collectives, per_device(): lax.all_to_all(routed[None], 'expert', split_axis=1, concat_axis=1, tiled...  17.1 us
    all_to_all x1, local copies, waits for them, and re-layouts, per_device(): lax.all_to_all(routed[None], 'expert', split_axis=1, concat_axis=1, tiled...  14.6 us
    broadcast_in_dim x1, other arithmetic, per_device(): fisher = (fisher_sum * (1.0 / (ways * groups_dev)))[None]  6.6 us
    all_to_all x1, starting transfers between devices, per_device(): lax.all_to_all(lax.all_to_all(routed[None], 'expert', split_axis=1, conca...  4.87 us
  transfers between devices with their start and end apart: 2, of which 0 were waited for; matrix products, arithmetic and copies ran while one was open for 29% of the time, Pallas kernels for 0%

commit v1 on v0

--- a/solution.py
+++ b/solution.py
@@ -27,13 +27,16 @@
         "jgec,jgd->ejcd", place.astype(jnp.bfloat16), token_rows, preferred_element_type=jnp.float32
     )
     routed = (picked * jnp.transpose(slot_gate, (1, 0, 2))[..., None]).astype(jnp.bfloat16)
-    columns = lax.all_to_all(
-        lax.all_to_all(routed[None], "expert", split_axis=1, concat_axis=1, tiled=True),
-        "dp",
-        split_axis=4,
-        concat_axis=0,
-        tiled=True,
+    keys_put = lambda xs: jnp.concatenate(
+        jax.lax.all_to_all(
+            jnp.stack(jnp.split(xs, jax.lax.axis_size("expert"), 1)),
+            concat_axis=0,
+            split_axis=0,
+            axis_name="expert",
+        ),
+        1,
     )
+    columns = lax.all_to_all(keys_put(routed[None]), "dp", split_axis=4, concat_axis=0, tiled=True)
     flat_cols = columns.reshape(-1, columns.shape[4])
     grad_rows = lax.psum_scatter(
         lax.dot_general(

time: 212 us -> 233 us (1.099)
  local copies, waits for them, and re-layouts: 70.2 us -> 90.4 us
    reshape x0 -> x1, local copies, waits for them, and re-layouts: none -> 24 us  [per_device(): jnp.concatenate(jax.lax.all_to_all(jnp.stack(jnp.split(xs, jax.lax.axis_s...]
    all_to_all x2 -> x1, local copies, waits for them, and re-layouts: 31.8 us -> 27.9 us  [per_device(): lax.all_to_all(keys_put(routed[None]), 'dp', split_axis=4, concat_axis=0,...]
  transfers between devices with their start and end apart: 2 -> 2, of which waited for: 0 -> 0; matrix products, arithmetic and copies ran while one was open for 29% -> 27% of each run, Pallas kernels for 0% -> 0%
where the time goes in v1:
time: 233 us; the launch traced here: 231 us
  local copies, waits for them, and re-layouts  90.4 us (39%)
  matrix products  62.3 us (27%)
  blocking collectives  49.5 us (21%)
  between operations  14.1 us (6%)
  other arithmetic  10.1 us (4%)
  starting transfers between devices  4.87 us (2%)
    dot_general x8, matrix products, turn(): lax.dot_general(block_h, block_c, (((0,), (0,)), ((), ())), preferred_ele...  55.4 us
    unnamed x4, local copies, waits for them, and re-layouts  38.2 us
    all_gather x1, blocking collectives, per_device(): piece = lax.all_gather(hidden, 'dp', axis=1, tiled=True)  32.4 us
    all_to_all x1, local copies, waits for them, and re-layouts, per_device(): lax.all_to_all(keys_put(routed[None]), 'dp', split_axis=4, concat_axis=0,...  27.9 us
    reshape x1, local copies, waits for them, and re-layouts, per_device(): jnp.concatenate(jax.lax.all_to_all(jnp.stack(jnp.split(xs, jax.lax.axis_s...  24 us
    all_to_all x1, blocking collectives, per_device(): jax.lax.all_to_all(jnp.stack(jnp.split(xs, jax.lax.axis_size('expert'), 1...  17.1 us
    broadcast_in_dim x1, other arithmetic, per_device(): fisher = (fisher_sum * (1.0 / (ways * groups_dev)))[None]  6.6 us
    all_to_all x1, starting transfers between devices, per_device(): lax.all_to_all(keys_put(routed[None]), 'dp', split_axis=4, concat_axis=0,...  4.87 us
  transfers between devices with their start and end apart: 2, of which 0 were waited for; matrix products, arithmetic and copies ran while one was open for 27% of the time, Pallas kernels for 0%

profile of v1, /device:TPU:0, one launch (start us, length us, event | category | flops | bytes accessed | tf_op | source)
XLA Modules:
  0.0 231.3 jit_solution(12038748967528284239)
XLA Ops:
  7.2 0.7 fusion.10
  7.9 0.1 copy.35
  8.1 0.2 reduce_window_sum.11
  8.3 0.1 copy.36
  8.4 0.7 select_reduce_fusion.1
  9.1 0.1 select_reduce_fusion
  9.2 2.6 %fusion.7 = bf16[1,4,2,8,7168]{4,3,1,2,0:T(8,128)(2,1)S(1)} fusion(bf16[2,128,7168,1]{2,1,3,0:T(8,128)(2,1)} %bitcast.64, f32[4,2,8]{2,0,1:T(4,128)S(1)} %bitcast.71, s32[2,128,4]{1,2,0:T(4,128)S(1)} %copy.36, pred[2,128,4]{1,2,0:T(4,128)(4,1)S(1)} %copy.37), kind=kOutput, calls=%fused_computation.9 | convolution fusion | flops 118374400 | bytes 4592896 | tf_op jit(solution)/shard_map/jgec,jgd->ejcd/dot_general | solution.py:26
  11.8 0.1 slice_bitcast_fusion.3
  11.9 0.1 pad_maximum_fusion
  12.0 17.1 %all_to_all.23 = bf16[4,1,1,2,8,7168]{5,4,3,2,1,0:T(8,128)(2,1)S(1)} all-to-all(bf16[4,1,1,2,8,7168]{5,4,3,2,1,0:T(8,128)(2,1)S(1)} %pad_maximum_fusion), channel_id=1, replica_groups=mesh['group'=2,'expert'=4,'dp'=4] {'expert'}, dimensions={0} | all-to-all | bytes 1835008 | tf_op jit(solution)/shard_map/all_to_all | solution.py:31
  29.1 24.0 %copy.41 = bf16[1,4,2,8,7168]{3,2,1,0,4:T(2,128)(2,1)} copy(bf16[1,4,2,8,7168]{4,3,2,1,0:T(8,128)(2,1)S(1)} %bitcast.65) | data formatting | bytes 1835008 | tf_op jit(solution)/shard_map/reshape | solution.py:30
  53.1 18.8 %reshape.83 = bf16[4,2,57344]{2,1,0:T(2,128)(2,1)} reshape(bf16[7168,1,4,2,8]{4,3,2,1,0:T(2,128)(2,1)} %bitcast.62) | data formatting | bytes 1835008
  71.9 4.9 %all-to-all-start.1 = ((bf16[4,2,57344]{2,1,0:T(2,128)(2,1)}), bf16[4,2,57344]{2,1,0:T(2,128)(2,1)S(1)}, u32[]{:S(2)}, u32[]{:S(2)}) async-start(bf16[4,2,57344]{2,1,0:T(2,128)(2,1)} %reshape.83), calls=%async_computation.1 | async-start | bytes 1835008 | tf_op jit(solution)/shard_map/all_to_all | solution.py:39
  76.8 0.0 reduce-scatter.2.cloned.1.call-start
  76.8 0.0 copy-done
  76.8 32.4 %all_gather.3 = bf16[1,4,4,2,8,1024]{5,4,3,2,0,1:T(8,128)(2,1)S(1)} all-gather(bf16[1,1,4,2,8,1024]{5,4,3,2,0,1:T(8,128)(2,1)S(1)} %bitcast.69), channel_id=1, replica_groups=mesh['group'=2,'expert'=4,'dp'=4] {'dp'}, dimensions={1}, use_global_device_ids=true | all-gather | bytes 655360 | tf_op jit(solution)/shard_map/all_gather | solution.py:52
  109.2 0.0 all-to-all-done.1
  109.2 19.4 %reshape.84 = bf16[7168,1,4,2,8]{4,3,2,1,0:T(2,128)(2,1)} reshape(bf16[4,2,57344]{2,1,0:T(2,128)(2,1)S(1)} %all-to-all-done.1) | data formatting | bytes 1835008
  128.6 27.9 %copy.42 = bf16[1,4,2,8,4,1792]{5,3,2,1,4,0:T(8,128)(2,1)S(1)} copy(bf16[1,4,2,8,4,1792]{3,2,1,5,4,0:T(2,128)(2,1)} %bitcast.63) | data formatting | bytes 1835008 | tf_op jit(solution)/shard_map/all_to_all | solution.py:39
  156.5 4.2 %fusion.8 = f32[256,1024]{1,0:T(8,128)} fusion(bf16[256,1792]{1,0:T(8,128)(2,1)S(1)} %bitcast.66, bf16[1,1024,1792]{2,1,0:T(8,128)(2,1)} %param.11), kind=kOutput, calls=%fused_computation.11 | convolution fusion | flops 939524096 | bytes 5636096 | tf_op jit(solution)/shard_map/dot_general | solution.py:42
  160.7 0.0 reduce-scatter.2.cloned.1.call-update
  160.7 55.5 %while.17 = (s32[]{:T(128)}, f32[1024,1792]{1,0:T(8,128)}, bf16[1,4,4,2,8,1024]{5,4,3,2,1,0:T(8,128)(2,1)S(1)}, bf16[4,4,2,8,1792]{4,3,2,1,0:T(8,128)(2,1)S(1)},...) while((s32[]{:T(128)}, f32[1024,1792]{1,0:T(8,128)}, ...), condition=%wide.region_5.6_spmd.clone, body=%wide.region_4.5_spmd.clone.sunk | while | flops 122945560 | bytes 14863173 | solution.py:71
  160.7 4.2 %select_add_fusion.2 = f32[1024,1792]{1,0:T(8,128)} fusion(f32[1024,1792]{1,0:T(8,128)} %get-tuple-element.212, pred[]{:T(512)S(6)} %compare.16, bf16[4,4,2,8,1792]{4,3,2,1,0:T(8,128)(2,1)S(1)} %get-tuple-element.224, s32[]{:T(128)S(6)} %select_n.92, s32[]{:T(128)S(6)} %select_n.95, bf16[1,4,4,2,8,1024]{5,4,3,2,1,0:T(8,128)(2,1)S(1)} %get-tuple-element.223), kind=kOutput, calls=%fused_computation.clone.1 | convolution fusion | flops 122945536 | bytes 14862848 | tf_op jit(solution)/shard_map/while/body/eval_jaxpr/dot_general | solution.py:66
  165.0 7.4 %select_add_fusion.2 = f32[1024,1792]{1,0:T(8,128)} fusion(f32[1024,1792]{1,0:T(8,128)} %get-tuple-element.212, pred[]{:T(512)S(6)} %compare.16, bf16[4,4,2,8,1792]{4,3,2,1,0:T(8,128)(2,1)S(1)} %get-tuple-element.224, s32[]{:T(128)S(6)} %select_n.92, s32[]{:T(128)S(6)} %select_n.95, bf16[1,4,4,2,8,1024]{5,4,3,2,1,0:T(8,128)(2,1)S(1)} %get-tuple-element.223), kind=kOutput, calls=%fused_computation.clone.1 | convolution fusion | flops 122945536 | bytes 14862848 | tf_op jit(solution)/shard_map/while/body/eval_jaxpr/dot_general | solution.py:66
  172.4 7.3 %select_add_fusion.2 = f32[1024,1792]{1,0:T(8,128)} fusion(f32[1024,1792]{1,0:T(8,128)} %get-tuple-element.212, pred[]{:T(512)S(6)} %compare.16, bf16[4,4,2,8,1792]{4,3,2,1,0:T(8,128)(2,1)S(1)} %get-tuple-element.224, s32[]{:T(128)S(6)} %select_n.92, s32[]{:T(128)S(6)} %select_n.95, bf16[1,4,4,2,8,1024]{5,4,3,2,1,0:T(8,128)(2,1)S(1)} %get-tuple-element.223), kind=kOutput, calls=%fused_computation.clone.1 | convolution fusion | flops 122945536 | bytes 14862848 | tf_op jit(solution)/shard_map/while/body/eval_jaxpr/dot_general | solution.py:66
  179.7 7.3 %select_add_fusion.2 = f32[1024,1792]{1,0:T(8,128)} fusion(f32[1024,1792]{1,0:T(8,128)} %get-tuple-element.212, pred[]{:T(512)S(6)} %compare.16, bf16[4,4,2,8,1792]{4,3,2,1,0:T(8,128)(2,1)S(1)} %get-tuple-element.224, s32[]{:T(128)S(6)} %select_n.92, s32[]{:T(128)S(6)} %select_n.95, bf16[1,4,4,2,8,1024]{5,4,3,2,1,0:T(8,128)(2,1)S(1)} %get-tuple-element.223), kind=kOutput, calls=%fused_computation.clone.1 | convolution fusion | flops 122945536 | bytes 14862848 | tf_op jit(solution)/shard_map/while/body/eval_jaxpr/dot_general | solution.py:66
  187.0 7.3 %select_add_fusion.2 = f32[1024,1792]{1,0:T(8,128)} fusion(f32[1024,1792]{1,0:T(8,128)} %get-tuple-element.212, pred[]{:T(512)S(6)} %compare.16, bf16[4,4,2,8,1792]{4,3,2,1,0:T(8,128)(2,1)S(1)} %get-tuple-element.224, s32[]{:T(128)S(6)} %select_n.92, s32[]{:T(128)S(6)} %select_n.95, bf16[1,4,4,2,8,1024]{5,4,3,2,1,0:T(8,128)(2,1)S(1)} %get-tuple-element.223), kind=kOutput, calls=%fused_computation.clone.1 | convolution fusion | flops 122945536 | bytes 14862848 | tf_op jit(solution)/shard_map/while/body/eval_jaxpr/dot_general | solution.py:66
  194.4 7.3 %select_add_fusion.2 = f32[1024,1792]{1,0:T(8,128)} fusion(f32[1024,1792]{1,0:T(8,128)} %get-tuple-element.212, pred[]{:T(512)S(6)} %compare.16, bf16[4,4,2,8,1792]{4,3,2,1,0:T(8,128)(2,1)S(1)} %get-tuple-element.224, s32[]{:T(128)S(6)} %select_n.92, s32[]{:T(128)S(6)} %select_n.95, bf16[1,4,4,2,8,1024]{5,4,3,2,1,0:T(8,128)(2,1)S(1)} %get-tuple-element.223), kind=kOutput, calls=%fused_computation.clone.1 | convolution fusion | flops 122945536 | bytes 14862848 | tf_op jit(solution)/shard_map/while/body/eval_jaxpr/dot_general | solution.py:66
  201.6 7.3 %select_add_fusion.2 = f32[1024,1792]{1,0:T(8,128)} fusion(f32[1024,1792]{1,0:T(8,128)} %get-tuple-element.212, pred[]{:T(512)S(6)} %compare.16, bf16[4,4,2,8,1792]{4,3,2,1,0:T(8,128)(2,1)S(1)} %get-tuple-element.224, s32[]{:T(128)S(6)} %select_n.92, s32[]{:T(128)S(6)} %select_n.95, bf16[1,4,4,2,8,1024]{5,4,3,2,1,0:T(8,128)(2,1)S(1)} %get-tuple-element.223), kind=kOutput, calls=%fused_computation.clone.1 | convolution fusion | flops 122945536 | bytes 14862848 | tf_op jit(solution)/shard_map/while/body/eval_jaxpr/dot_general | solution.py:66
  208.9 7.3 %select_add_fusion.2 = f32[1024,1792]{1,0:T(8,128)} fusion(f32[1024,1792]{1,0:T(8,128)} %get-tuple-element.212, pred[]{:T(512)S(6)} %compare.16, bf16[4,4,2,8,1792]{4,3,2,1,0:T(8,128)(2,1)S(1)} %get-tuple-element.224, s32[]{:T(128)S(6)} %select_n.92, s32[]{:T(128)S(6)} %select_n.95, bf16[1,4,4,2,8,1024]{5,4,3,2,1,0:T(8,128)(2,1)S(1)} %get-tuple-element.223), kind=kOutput, calls=%fused_computation.clone.1 | convolution fusion | flops 122945536 | bytes 14862848 | tf_op jit(solution)/shard_map/while/body/eval_jaxpr/dot_general | solution.py:66
  216.2 6.6 %multiply_bitcast_fusion = f32[1,1024,1792]{2,1,0:T(8,128)} fusion(f32[1024,1792]{1,0:T(8,128)} %get-tuple-element.140), kind=kLoop, calls=%fused_computation.10 | loop fusion | flops 1835008 | bytes 14680064 | tf_op jit(solution)/shard_map/broadcast_in_dim | solution.py:72
  222.8 1.6 convert_element_type.26
  (8 shorter events, 0.0 us)
Async XLA Ops:
  53.1 23.7 %copy-start = (bf16[1,1,4,2,8,1024]{5,4,3,2,1,0:T(8,128)(2,1)S(1)}, bf16[1,1,4,2,8,1024]{5,4,3,2,1,0:T(8,128)(2,1)}, u32[]{:S(2)}) copy-start(bf16[1,1,4,2,8,1024]{5,4,3,2,1,0:T(8,128)(2,1)} %param.10) | copy-start | bytes 393220
  71.9 37.3 %all-to-all-start.1 = ((bf16[4,2,57344]{2,1,0:T(2,128)(2,1)}), bf16[4,2,57344]{2,1,0:T(2,128)(2,1)S(1)}, u32[]{:S(2)}, u32[]{:S(2)}) async-start(bf16[4,2,57344]{2,1,0:T(2,128)(2,1)} %reshape.83), calls=%async_computation.1 | async-start | bytes 1835008 | tf_op jit(solution)/shard_map/all_to_all | solution.py:39
  76.8 146.0 %reduce-scatter.2.cloned.1.call-start = ((), (), s32[]{:S(2)}) async-start(), calls=%async_computation.3 | async-start | bytes 1310720 | tf_op jit(solution)/shard_map/reduce_scatter | solution.py:41
Sparse Core Ops, SparseCore 0:
  160.8 27.8 reduce-scatter.1
